TPU v7x, 128 devices: a whole 4x4x4 slice. The times are simulated.
128 devices in a mesh: blk: 16 (over z, y_hi, core), uly: 8 (over x, y_lo).
Axes of the slice: x: 4, y: 4 (y_hi: 2, y_lo: 2; y = y_hi * 2 + y_lo), z: 4, core: 2. Of those that a mesh axis runs over, the one named last changes fastest.
Arguments:
- queries: bfloat16 [128, 192, 8192], P(('blk', 'uly')), may hold values from -4 to 4
- own_keys: bfloat16 [128, 192, 1024], P(('blk', 'uly')), may hold values from -12 to 12
- own_values: bfloat16 [128, 192, 1024], P(('blk', 'uly')), may hold values from -6 to 6
- key_codes: bfloat16 [2048, 1024], P('blk', 'uly'), may hold values from -128 to 128
- value_codes: bfloat16 [2048, 1024], P('blk', 'uly'), may hold values from -6 to 6
- code_scales: bfloat16 [2048, 8, 2], P('blk', 'uly'), may hold values from 0.5 to 2
- lengths: int32 [128], P(('blk', 'uly')), may hold values from 1 to 192, as said below
Outputs:
- attention_out: bfloat16 [128, 192, 8192], P(('blk', 'uly'))
Inputs may be any that keep to these rules, and one draw needn't show every extreme that they name: `lengths`: one response in every draw has exactly 192 tokens.
All inputs are finite; a program needn't handle non-finite values.
Results may differ from a plain program's by a relative error of at most 0.0056.
Values may be sent and summed in bfloat16 or wider, within the bound.
A program may use at most 192 MiB of HBM per device.

v0:
```python
from functools import partial
import math

import jax
import jax.numpy as jnp
from jax import lax
from jax.sharding import PartitionSpec as P

D_HEAD = 128


def empty_state(responses, length, groups, group_size):
    leading = (responses, groups, group_size, length)
    return (
        jnp.full(leading, -jnp.inf, jnp.float32),
        jnp.zeros(leading, jnp.float32),
        jnp.zeros(leading + (D_HEAD,), jnp.float32),
    )


def fold_scores(running, scores, allowed):
    highest, totals, accumulated = running
    if allowed is None:
        masked = scores
    else:
        masked = jnp.where(allowed, scores, -jnp.inf)
    new_high = jnp.maximum(highest, jnp.max(masked, axis=-1))
    shrink = jnp.exp(highest - new_high)
    weights = jnp.exp(masked - new_high[..., None])
    totals = totals * shrink + jnp.sum(weights, axis=-1)
    return (new_high, totals, shrink, weights.astype(jnp.bfloat16))


def dequantize(code_rows, factors):
    positions = code_rows.shape[0]
    groups = factors.shape[1]
    widened = code_rows.astype(jnp.float32).reshape(positions, groups, -1)
    return (widened * factors.astype(jnp.float32)[:, :, None]).astype(jnp.bfloat16)


def prompt_step(running, block_rows, grouped, scaling):
    key_rows, value_rows, scale_rows = block_rows
    prompt_keys = dequantize(key_rows, scale_rows[:, :, 0])
    prompt_values = dequantize(value_rows, scale_rows[:, :, 1])
    scores = (
        jnp.einsum("rtkgd,nkd->rkgtn", grouped, prompt_keys, preferred_element_type=jnp.float32)
        * scaling
    )
    new_high, totals, shrink, weights = fold_scores(running, scores, None)
    accumulated = running[2] * shrink[..., None] + jnp.einsum(
        "rkgtn,nkd->rkgtd", weights, prompt_values, preferred_element_type=jnp.float32
    )
    return (new_high, totals, accumulated)


def fold_prompt(running, shard_piece, first_row, grouped, scaling, target):
    key_rows, value_rows, scale_rows = shard_piece
    positions = key_rows.shape[0]
    step_rows = math.gcd(positions, target)
    blocks_count = positions // step_rows
    stacked = (
        key_rows.reshape(blocks_count, step_rows, key_rows.shape[1]),
        value_rows.reshape(blocks_count, step_rows, value_rows.shape[1]),
        scale_rows.reshape(blocks_count, step_rows, scale_rows.shape[1], 2),
    )

    def advance(running_now, block_rows):
        return (prompt_step(running_now, block_rows, grouped, scaling), None)

    final_state, unused = lax.scan(advance, running, stacked)
    return final_state


def own_step(running, grouped, keys_here, values_here, scaling):
    length = grouped.shape[1]
    scores = (
        jnp.einsum("rtkgd,rjkd->rkgtj", grouped, keys_here, preferred_element_type=jnp.float32)
        * scaling
    )
    tokens = lax.broadcasted_iota(jnp.int32, (length, length), 0)
    sources = lax.broadcasted_iota(jnp.int32, (length, length), 1)
    new_high, totals, shrink, weights = fold_scores(running, scores, tokens >= sources)
    accumulated = running[2] * shrink[..., None] + jnp.einsum(
        "rkgtj,rjkd->rkgtd", weights, values_here, preferred_element_type=jnp.float32
    )
    return (new_high, totals, accumulated)


def with_own(fold_call, grouped, keys_here, values_here, scaling):
    responses = grouped.shape[0]
    length = grouped.shape[1]
    initial = empty_state(responses, length, grouped.shape[2], grouped.shape[3])
    return own_step(fold_call(initial), grouped, keys_here, values_here, scaling)


def finish(final_state):
    highest, totals, accumulated = final_state
    attended = accumulated / totals[..., None]
    responses = attended.shape[0]
    length = attended.shape[3]
    heads_here = attended.shape[1] * attended.shape[2]
    return (
        jnp.transpose(attended, (0, 3, 1, 2, 4))
        .reshape(responses, length, heads_here * D_HEAD)
        .astype(jnp.bfloat16)
    )


def body(queries, own_keys, own_values, key_codes, value_codes, code_scales, lengths):
    scaling = 1.0 / math.sqrt(D_HEAD)
    length = queries.shape[1]
    uly_count = lax.axis_size("uly")
    local_heads = queries.shape[2] // D_HEAD // uly_count
    local_groups = own_keys.shape[2] // D_HEAD // uly_count
    group_size = local_heads // local_groups
    head_queries, head_keys, head_values = (
        lax.all_to_all(queries, "uly", split_axis=2, concat_axis=0, tiled=True),
        lax.all_to_all(own_keys, "uly", split_axis=2, concat_axis=0, tiled=True),
        lax.all_to_all(own_values, "uly", split_axis=2, concat_axis=0, tiled=True),
    )
    responses = head_queries.shape[0]
    grouped = head_queries.reshape(responses, length, local_groups, group_size, D_HEAD)
    keys_here = head_keys.reshape(responses, length, local_groups, D_HEAD)
    values_here = head_values.reshape(responses, length, local_groups, D_HEAD)
    fold_step = partial(fold_prompt, grouped=grouped, scaling=scaling, target=1024)

    def fold_call(starting):
        return fold_step(
            starting,
            (
                lax.all_gather(key_codes, "blk", axis=0, tiled=True),
                lax.all_gather(value_codes, "blk", axis=0, tiled=True),
                lax.all_gather(code_scales, "blk", axis=0, tiled=True),
            ),
            jnp.int32(0),
        )

    ordered = finish(with_own(fold_call, grouped, keys_here, values_here, scaling))
    returned = lax.all_to_all(ordered, "uly", split_axis=0, concat_axis=2, tiled=True)
    tokens = lax.broadcasted_iota(jnp.int32, (returned.shape[0], length), 1)
    return jnp.where((tokens < lengths[:, None])[..., None], returned, jnp.zeros_like(returned))


def solution(mesh):
    placed = (
        P(("blk", "uly"), None, None),
        P(("blk", "uly"), None, None),
        P(("blk", "uly"), None, None),
        P("blk", "uly"),
        P("blk", "uly"),
        P("blk", "uly", None),
        P(("blk", "uly")),
    )
    return jax.shard_map(
        body, mesh=mesh, in_specs=placed, out_specs=P(("blk", "uly"), None, None), check_vma=False
    )
```

profile of v0, /device:TPU:1, one launch (start us, length us, event | category | flops | bytes accessed | tf_op | source)
XLA Modules:
  0.0 467.5 jit_solution(5643050089154257334)
XLA Ops:
  8.2 5.9 %all-to-all-start.1 = ((bf16[8,2,12288]{2,1,0:T(2,128)(2,1)}), bf16[8,2,12288]{2,1,0:T(2,128)(2,1)S(1)}, u32[]{:S(2)}, u32[]{:S(2)}) async-start(bf16[8,2,12288]{2,1,0:T(2,128)(2,1)} %reshape.265), calls=%async_computation.1 | async-start | bytes 786432 | tf_op jit(solution)/shard_map/all_to_all | solution.py:118
  16.4 3.9 reduce.6
  21.8 5.6 %all-to-all-start.2 = ((bf16[8,2,12288]{2,1,0:T(2,128)(2,1)}), bf16[8,2,12288]{2,1,0:T(2,128)(2,1)S(1)}, u32[]{:S(2)}, u32[]{:S(2)}) async-start(bf16[8,2,12288]{2,1,0:T(2,128)(2,1)} %reshape.267), calls=%async_computation.2 | async-start | bytes 786432 | tf_op jit(solution)/shard_map/all_to_all | solution.py:119
  27.4 17.6 %copy.37 = bf16[1,192,8192]{1,0,2:T(2,128)(2,1)} copy(bf16[1,192,8192]{2,1,0:T(8,128)(2,1)} %param.9) | data formatting | bytes 6291456 | tf_op args[0]
  45.1 47.5 %reduce.4 = bf16[8192,192]{1,0:T(8,128)(2,1)} reduce(bf16[8192,1,192]{2,1,0:T(2,128)(2,1)} %bitcast.223, bf16[]{:T(256)} %broadcast.129), dimensions={1}, to_apply=%bitcast.171.reduce_sub_computation | reduce | bytes 6291458
  92.6 8.7 %reshape.263 = bf16[8,2,98304]{2,1,0:T(2,128)(2,1)} reshape(bf16[8192,192]{1,0:T(8,128)(2,1)} %reduce.4) | data formatting | bytes 6291456
  102.1 5.1 %all-to-all-start = ((bf16[8,2,98304]{2,1,0:T(2,128)(2,1)}), bf16[8,2,98304]{2,1,0:T(2,128)(2,1)S(1)}, u32[]{:S(2)}, u32[]{:S(2)}) async-start(bf16[8,2,98304]{2,1,0:T(2,128)(2,1)} %reshape.263), calls=%async_computation | async-start | bytes 6291456 | tf_op jit(solution)/shard_map/all_to_all | solution.py:117
  107.3 44.6 %all_gather.10 = bf16[2048,1,2]{0,2,1:T(2,128)(2,1)S(1)} all-gather(bf16[128,1,2]{0,2,1:T(2,128)(2,1)S(1)} %copy-done.12), channel_id=1, replica_groups=mesh['blk'=16,'uly'=8] {'blk'}, dimensions={0}, use_global_device_ids=true | all-gather | bytes 8704 | tf_op jit(solution)/shard_map/all_gather | solution.py:133
  152.5 25.5 %all_gather.9 = bf16[2048,128]{1,0:T(8,128)(2,1)} all-gather(bf16[128,128]{1,0:T(8,128)(2,1)S(1)} %copy-done.10), channel_id=1, replica_groups=mesh['blk'=16,'uly'=8] {'blk'}, dimensions={0}, use_global_device_ids=true | all-gather | bytes 557056 | tf_op jit(solution)/shard_map/all_gather | solution.py:131
  178.0 23.1 %all_gather.11 = bf16[2048,128]{1,0:T(8,128)(2,1)} all-gather(bf16[128,128]{1,0:T(8,128)(2,1)S(1)} %copy-done.11), channel_id=1, replica_groups=mesh['blk'=16,'uly'=8] {'blk'}, dimensions={0}, use_global_device_ids=true | all-gather | bytes 557056 | tf_op jit(solution)/shard_map/all_gather | solution.py:132
  216.4 7.5 %reshape.264 = bf16[8192,1,192]{2,1,0:T(2,128)(2,1)} reshape(bf16[8,2,98304]{2,1,0:T(2,128)(2,1)S(1)} %all-to-all-done) | data formatting | bytes 6291456
  224.0 18.3 %copy.38 = bf16[1,192,8192]{2,1,0:T(8,128)(2,1)S(1)} copy(bf16[1,192,8192]{1,0,2:T(2,128)(2,1)} %bitcast.224) | data formatting | bytes 6291456 | tf_op jit(solution)/shard_map/all_to_all | solution.py:117
  251.4 122.0 %while.15 = (s32[]{:T(128)}, f32[8,1,8,192]{3,2,0,1:T(8,128)S(1)}, f32[8,1,8,192]{3,2,0,1:T(8,128)S(1)}, f32[8,1,8,192,128]{4,3,2,0,1:T(8,128)}, bf16[2,1024,128...) while((s32[]{:T(128)}, f32[8,1,8,192]{3,2,0,1:T(8,128)S(1)}, ...), condition=%wide.region_3.4_spmd.clone, body=%wide.region_0.3_spmd.clone.sunk | while | flops 6548695040 | bytes 218427584 | solution.py:70
  251.6 21.4 %bitcast_reduce_fusion.2 = (f32[8,8,192]{2,1,0:T(8,128)S(1)}, f32[1024,8,192,8]{0,2,3,1:T(8,128)}) fusion(bf16[8,192,1,8,128]{4,1,3,0,2:T(8,128)(2,1)} %get-tuple-element.226, f32[1024]{0:T(1024)S(1)} %bitcast.240, bf16[2,1024,128]{2,1,0:T(8,128)(2,1)S(1)} %get-tuple-element.224, s32[]{:T(128)S(6)} %copy.82), kind=kOutput, calls=%fused_computation.1.clone.1 | convolution fusion | flops 3246772224 | bytes 53792772 | tf_op jit(solution)/shard_map/while/body/eval_jaxpr/rtkgd,nkd->rkgtn/dot_general | solution.py:46
  273.0 16.5 %fusion.59 = f32[8,8,192]{2,1,0:T(8,128)S(1)} fusion(f32[1024,8,192,8]{0,2,3,1:T(8,128)} %get-tuple-element.197, f32[8,8,192]{2,1,0:T(8,128)S(1)} %bitcast.221), kind=kLoop, calls=%fused_computation.4.clone.1 | loop fusion | flops 37736448 | bytes 50429952 | tf_op jit(solution)/shard_map/while/body/eval_jaxpr/reduce_sum | solution.py:30
  290.2 19.6 %bitcast_add_fusion.7 = f32[8,1,8,192,128]{4,3,2,0,1:T(8,128)S(1)} fusion(f32[8,1,8,192,128]{4,3,2,0,1:T(8,128)S(1)} %copy-done, f32[8,8,192]{2,1,0:T(8,128)S(1)} %get-tuple-element.198, pred[]{:T(512)S(6)} %compare.3, f32[1024,8,192,8]{0,2,3,1:T(8,128)} %get-tuple-element.197, f32[8,8,192]{2,1,0:T(8,128)S(1)} %bitcast.222, f32[1024]{0:T(1024)S(1)} %bitcast.239, ...), kind=kOutput, calls=%fused_computation.9.clone.1 | convolution fusion | flops 3264086016 | bytes 63311876 | tf_op jit(solution)/shard_map/while/body/eval_jaxpr/rkgtn,nkd->rkgtd/dot_general | solution.py:50
  312.4 21.4 %bitcast_reduce_fusion.2 = (f32[8,8,192]{2,1,0:T(8,128)S(1)}, f32[1024,8,192,8]{0,2,3,1:T(8,128)}) fusion(bf16[8,192,1,8,128]{4,1,3,0,2:T(8,128)(2,1)} %get-tuple-element.226, f32[1024]{0:T(1024)S(1)} %bitcast.240, bf16[2,1024,128]{2,1,0:T(8,128)(2,1)S(1)} %get-tuple-element.224, s32[]{:T(128)S(6)} %copy.82), kind=kOutput, calls=%fused_computation.1.clone.1 | convolution fusion | flops 3246772224 | bytes 53792772 | tf_op jit(solution)/shard_map/while/body/eval_jaxpr/rtkgd,nkd->rkgtn/dot_general | solution.py:46
  333.8 16.5 %fusion.59 = f32[8,8,192]{2,1,0:T(8,128)S(1)} fusion(f32[1024,8,192,8]{0,2,3,1:T(8,128)} %get-tuple-element.197, f32[8,8,192]{2,1,0:T(8,128)S(1)} %bitcast.221), kind=kLoop, calls=%fused_computation.4.clone.1 | loop fusion | flops 37736448 | bytes 50429952 | tf_op jit(solution)/shard_map/while/body/eval_jaxpr/reduce_sum | solution.py:30
  351.0 19.6 %bitcast_add_fusion.7 = f32[8,1,8,192,128]{4,3,2,0,1:T(8,128)S(1)} fusion(f32[8,1,8,192,128]{4,3,2,0,1:T(8,128)S(1)} %copy-done, f32[8,8,192]{2,1,0:T(8,128)S(1)} %get-tuple-element.198, pred[]{:T(512)S(6)} %compare.3, f32[1024,8,192,8]{0,2,3,1:T(8,128)} %get-tuple-element.197, f32[8,8,192]{2,1,0:T(8,128)S(1)} %bitcast.222, f32[1024]{0:T(1024)S(1)} %bitcast.239, ...), kind=kOutput, calls=%fused_computation.9.clone.1 | convolution fusion | flops 3264086016 | bytes 63311876 | tf_op jit(solution)/shard_map/while/body/eval_jaxpr/rkgtn,nkd->rkgtd/dot_general | solution.py:50
  373.4 11.3 %fusion.30 = (f32[8,8,192]{2,1,0:T(8,128)S(1)}, f32[8,192,192,8]{2,1,3,0:T(8,128)}) fusion(pred[192,192]{0,1:T(8,128)(4,1)S(1)} %copy-done.8, bf16[8,192,8,128]{3,2,0,1:T(8,128)(2,1)} %bitcast.226, bf16[1,192,8,128]{3,1,2,0:T(8,128)(2,1)} %copy.43), kind=kOutput, calls=%fused_computation.40 | convolution fusion | flops 611045376 | bytes 13062144 | tf_op jit(solution)/shard_map/rtkgd,rjkd->rkgtj/dot_general | solution.py:77
  384.6 7.7 %fusion.28 = f32[8,8,192]{2,1,0:T(8,128)S(1)} fusion(f32[8,192,192,8]{2,1,3,0:T(8,128)} %get-tuple-element.138, f32[8,8,192]{2,1,0:T(8,128)S(1)} %fusion.48, pred[192,192]{0,1:T(8,128)(4,1)S(1)} %copy-done.8), kind=kLoop, calls=%fused_computation.38 | loop fusion | flops 9424896 | bytes 9572352 | tf_op jit(solution)/shard_map/reduce_sum | solution.py:30
  392.4 8.8 %fusion.42 = bf16[8,192,1,8,128]{4,1,3,0,2:T(8,128)(2,1)S(1)} fusion(f32[8,8,192]{2,1,0:T(8,128)S(1)} %get-tuple-element.136, f32[8,1,8,192,128]{4,3,2,0,1:T(8,128)S(1)} %copy-done.2, f32[8,8,192]{2,1,0:T(8,128)S(1)} %get-tuple-element.135, f32[8,192,192,8]{2,1,3,0:T(8,128)} %get-tuple-element.138, f32[8,8,192]{2,1,0:T(8,128)S(1)} %fusion.48, ...), kind=kOutput, calls=%fused_computation.53 | convolution fusion | flops 619708416 | bytes 19451904 | tf_op jit(solution)/shard_map/rkgtj,rjkd->rkgtd/dot_general | solution.py:83
  406.5 13.3 %all-to-all-start.3 = ((bf16[8,192,1024]{2,1,0:T(8,128)(2,1)}), bf16[8,192,1024]{2,1,0:T(8,128)(2,1)S(1)}, u32[]{:S(2)}, u32[]{:S(2)}) async-start(bf16[8,192,1024]{2,1,0:T(8,128)(2,1)} %convert_element_type.118), calls=%async_computation.3 | async-start | bytes 6291456 | tf_op jit(solution)/shard_map/all_to_all | solution.py:139
  420.5 44.5 %all-to-all-done.3 = bf16[8,192,1024]{2,1,0:T(8,128)(2,1)S(1)} async-done(((bf16[8,192,1024]{2,1,0:T(8,128)(2,1)}), bf16[8,192,1024]{2,1,0:T(8,128)(2,1)S(1)}, u32[]{:S(2)}, u32[]{:S(2)}) %all-to-all-start.3) | async-done | bytes 3145760 | tf_op jit(solution)/shard_map/all_to_all | solution.py:139
  (70 shorter events, 52.1 us)
Async XLA Ops:
  8.2 13.6 %all-to-all-start.1 = ((bf16[8,2,12288]{2,1,0:T(2,128)(2,1)}), bf16[8,2,12288]{2,1,0:T(2,128)(2,1)S(1)}, u32[]{:S(2)}, u32[]{:S(2)}) async-start(bf16[8,2,12288]{2,1,0:T(2,128)(2,1)} %reshape.265), calls=%async_computation.1 | async-start | bytes 786432 | tf_op jit(solution)/shard_map/all_to_all | solution.py:118
  21.8 70.8 %copy-start.6 = (bf16[8,2,12288]{2,1,0:T(2,128)(2,1)}, bf16[8,2,12288]{2,1,0:T(2,128)(2,1)S(1)}, u32[]{:S(2)}) copy-start(bf16[8,2,12288]{2,1,0:T(2,128)(2,1)S(1)} %all-to-all-done.1) | copy-start | bytes 1179652
  21.8 79.6 %all-to-all-start.2 = ((bf16[8,2,12288]{2,1,0:T(2,128)(2,1)}), bf16[8,2,12288]{2,1,0:T(2,128)(2,1)S(1)}, u32[]{:S(2)}, u32[]{:S(2)}) async-start(bf16[8,2,12288]{2,1,0:T(2,128)(2,1)} %reshape.267), calls=%async_computation.2 | async-start | bytes 786432 | tf_op jit(solution)/shard_map/all_to_all | solution.py:119
  92.6 14.7 %copy-start.12 = (bf16[128,1,2]{0,2,1:T(2,128)(2,1)S(1)}, bf16[128,1,2]{0,2,1:T(2,128)(2,1)}, u32[]{:S(2)}) copy-start(bf16[128,1,2]{0,2,1:T(2,128)(2,1)} %param.14) | copy-start | bytes 1540
  92.6 59.9 %copy-start.10 = (bf16[128,128]{1,0:T(8,128)(2,1)S(1)}, bf16[128,128]{1,0:T(8,128)(2,1)}, u32[]{:S(2)}) copy-start(bf16[128,128]{1,0:T(8,128)(2,1)} %param.12) | copy-start | bytes 98308
  92.6 85.4 %copy-start.11 = (bf16[128,128]{1,0:T(8,128)(2,1)S(1)}, bf16[128,128]{1,0:T(8,128)(2,1)}, u32[]{:S(2)}) copy-start(bf16[128,128]{1,0:T(8,128)(2,1)} %param.13) | copy-start | bytes 98308
  101.4 0.7 copy-start.7
  102.1 114.3 %all-to-all-start = ((bf16[8,2,98304]{2,1,0:T(2,128)(2,1)}), bf16[8,2,98304]{2,1,0:T(2,128)(2,1)S(1)}, u32[]{:S(2)}, u32[]{:S(2)}) async-start(bf16[8,2,98304]{2,1,0:T(2,128)(2,1)} %reshape.263), calls=%async_computation | async-start | bytes 6291456 | tf_op jit(solution)/shard_map/all_to_all | solution.py:117
  245.2 6.2 %copy-start.4 = (bf16[2048,128]{1,0:T(8,128)(2,1)S(1)}, bf16[2048,128]{1,0:T(8,128)(2,1)}, u32[]{:S(2)}) copy-start(bf16[2048,128]{1,0:T(8,128)(2,1)} %all_gather.9) | copy-start | bytes 1572868
  245.2 6.2 %copy-start.5 = (bf16[2048,128]{1,0:T(8,128)(2,1)S(1)}, bf16[2048,128]{1,0:T(8,128)(2,1)}, u32[]{:S(2)}) copy-start(bf16[2048,128]{1,0:T(8,128)(2,1)} %all_gather.11) | copy-start | bytes 1572868
  246.0 1.7 copy-start.3
  251.4 122.0 %copy-start.8 = (pred[192,192]{0,1:T(8,128)(4,1)S(1)}, pred[192,192]{0,1:T(8,128)(4,1)}, u32[]{:S(2)}) copy-start(pred[192,192]{0,1:T(8,128)(4,1)} %iota_compare_fusion) | copy-start | bytes 110596
  273.0 17.2 %copy-start = (f32[8,1,8,192,128]{4,3,2,0,1:T(8,128)S(1)}, f32[8,1,8,192,128]{4,3,2,0,1:T(8,128)}, u32[]{:S(2)}) copy-start(f32[8,1,8,192,128]{4,3,2,0,1:T(8,128)} %get-tuple-element.213) | copy-start | bytes 18874372 | tf_op jit(solution)/shard_map/while
  309.8 2.6 copy-start.1
  333.8 17.2 %copy-start = (f32[8,1,8,192,128]{4,3,2,0,1:T(8,128)S(1)}, f32[8,1,8,192,128]{4,3,2,0,1:T(8,128)}, u32[]{:S(2)}) copy-start(f32[8,1,8,192,128]{4,3,2,0,1:T(8,128)} %get-tuple-element.213) | copy-start | bytes 18874372 | tf_op jit(solution)/shard_map/while
  370.6 2.6 copy-start.1
  384.6 7.8 %copy-start.2 = (f32[8,1,8,192,128]{4,3,2,0,1:T(8,128)S(1)}, f32[8,1,8,192,128]{4,3,2,0,1:T(8,128)}, u32[]{:S(2)}) copy-start(f32[8,1,8,192,128]{4,3,2,0,1:T(8,128)} %get-tuple-element.49) | copy-start | bytes 18874372
  384.6 7.8 %copy-start.9 = (bf16[1,192,8,128]{3,1,2,0:T(8,128)(2,1)S(1)}, bf16[1,192,8,128]{3,1,2,0:T(8,128)(2,1)}, u32[]{:S(2)}) copy-start(bf16[1,192,8,128]{3,1,2,0:T(8,128)(2,1)} %copy.48) | copy-start | bytes 1179652
  406.5 58.4 %all-to-all-start.3 = ((bf16[8,192,1024]{2,1,0:T(8,128)(2,1)}), bf16[8,192,1024]{2,1,0:T(8,128)(2,1)S(1)}, u32[]{:S(2)}, u32[]{:S(2)}) async-start(bf16[8,192,1024]{2,1,0:T(8,128)(2,1)} %convert_element_type.118), calls=%async_computation.3 | async-start | bytes 6291456 | tf_op jit(solution)/shard_map/all_to_all | solution.py:139
where the time goes:
time: 476 us; the launch traced here: 468 us
  matrix products  102 us (21%)
  other arithmetic  98.8 us (21%)
  local copies, waits for them, and re-layouts  97.6 us (21%)
  blocking collectives  93.2 us (20%)
  waiting for transfers between devices  44.5 us (9%)
  starting transfers between devices  29.9 us (6%)
    unnamed x38, local copies, waits for them, and re-layouts  63 us
    unnamed x6, other arithmetic  55.4 us
    all_gather x1, blocking collectives, fold_call(): lax.all_gather(code_scales, 'blk', axis=0, tiled=True)  44.6 us
    all_to_all x1, waiting for transfers between devices, body(): lax.all_to_all(ordered, 'uly', split_axis=0, concat_axis=2, tiled=True)  44.5 us
    dot_general x2, matrix products, prompt_step(): jnp.einsum('rtkgd,nkd->rkgtn', grouped, prompt_keys, preferred_element_ty...  42.9 us
    reduce_sum x3, other arithmetic, fold_scores(): totals = totals * shrink + jnp.sum(weights, axis=-1)  40.7 us
    dot_general x2, matrix products, prompt_step(): jnp.einsum('rkgtn,nkd->rkgtd', weights, prompt_values, preferred_element_...  39.1 us
    all_gather x1, blocking collectives, fold_call(): lax.all_gather(key_codes, 'blk', axis=0, tiled=True)  25.5 us
  transfers between devices with their start and end apart: 4, of which 1 were waited for; matrix products, arithmetic and copies ran while one was open for 21% of the time, Pallas kernels for 0%

commit v1 on v0

v1 whole, which is shorter than its diff:
```python
import math

import jax
import jax.numpy as jnp
from jax import lax
from jax.experimental import pallas as pl
from jax.experimental.pallas import tpu as pltpu
from jax.sharding import PartitionSpec as P

D = 128
HEADS_KV = 8
GROUP = 8
LENGTH = 192
BLOCKS = 16
PROMPT = 2048
CHUNK = 512
TOKENS = 64
HALF = 4
ROWS = HALF * TOKENS
SCALE = math.log2(math.e) / math.sqrt(D)


def dot_t(a, b):
    return lax.dot_general(a, b, (((1,), (1,)), ((), ())), preferred_element_type=jnp.float32)


def attend(lengths_ref, q_ref, kv_ref, ok_ref, ov_ref, o_ref, s_ref, m_ref, ovt_ref, mask_ref):
    key_at = lax.broadcasted_iota(jnp.int32, (TOKENS, ROWS), 0)
    token_at = lax.broadcasted_iota(jnp.int32, (TOKENS, ROWS), 1) % TOKENS
    mask_ref[...] = jnp.where(token_at >= key_at, 0.0, -jnp.inf).astype(jnp.float32)
    for g in range(HEADS_KV):
        turned = ov_ref[:, g * D : (g + 1) * D].T
        ovt_ref[g] = jnp.concatenate([turned, jnp.zeros((D, 256 - LENGTH), jnp.bfloat16)], axis=1)
    length = lengths_ref[0]
    per = CHUNK // D

    def columns(g, hh, h):
        return pl.ds(pl.multiple_of((g * GROUP + hh * HALF + h) * D, D), D)

    def scores(g, t, slot):
        hh, j = t // 3, t % 3
        q = jnp.concatenate([q_ref[j * TOKENS : (j + 1) * TOKENS, columns(g, hh, h)] for h in range(HALF)], axis=0)
        q = q.astype(jnp.float32) * SCALE
        high = q.astype(jnp.bfloat16)
        low = (q - high.astype(jnp.float32)).astype(jnp.bfloat16)
        q = jnp.concatenate([high, low], axis=1)
        top = jnp.full((8, ROWS), -jnp.inf, jnp.float32)
        for c in range(PROMPT // CHUNK):
            keys = jnp.concatenate([kv_ref[g * BLOCKS + c * per + b, :D] for b in range(per)], axis=0)
            s = dot_t(jnp.concatenate([keys, keys], axis=1), q)
            s_ref[slot, c * CHUNK : (c + 1) * CHUNK] = s
            top = jnp.maximum(top, jnp.max(s.reshape(CHUNK // 8, 8, ROWS), axis=0))
        n = (j + 1) * TOKENS
        keys = ok_ref[:n, pl.ds(pl.multiple_of(g * D, D), D)]
        s = dot_t(jnp.concatenate([keys, keys], axis=1), q)
        if j:
            s_ref[slot, PROMPT : PROMPT + j * TOKENS] = s[: j * TOKENS]
            top = jnp.maximum(top, jnp.max(s[: j * TOKENS].reshape(j * 8, 8, ROWS), axis=0))
        last = s[j * TOKENS :] + mask_ref[...]
        s_ref[slot, PROMPT + j * TOKENS : PROMPT + n] = last
        top = jnp.maximum(top, jnp.max(last.reshape(8, 8, ROWS), axis=0))
        m_ref[slot] = jnp.broadcast_to(jnp.max(top, axis=0, keepdims=True), (8, ROWS))

    def values(g, t, slot):
        hh, j = t // 3, t % 3
        top = m_ref[slot][:1]
        total = jnp.zeros((8, ROWS), jnp.float32)
        acc = jnp.zeros((D, ROWS), jnp.float32)
        for c in range(PROMPT // CHUNK):
            p = jnp.exp2(s_ref[slot, c * CHUNK : (c + 1) * CHUNK] - top)
            total = total + jnp.sum(p.reshape(CHUNK // 8, 8, ROWS), axis=0)
            turned = jnp.concatenate([kv_ref[g * BLOCKS + c * per + b, D:] for b in range(per)], axis=1)
            acc = acc + jnp.dot(turned, p.astype(jnp.bfloat16), preferred_element_type=jnp.float32)
        n = (j + 1) * TOKENS
        depth = 128 if j < 2 else 256
        p = jnp.exp2(s_ref[slot, PROMPT : PROMPT + n] - top)
        total = total + jnp.sum(p.reshape(n // 8, 8, ROWS), axis=0)
        p = p.astype(jnp.bfloat16)
        if depth > n:
            p = jnp.concatenate([p, jnp.zeros((depth - n, ROWS), jnp.bfloat16)], axis=0)
        acc = acc + jnp.dot(ovt_ref[g, :, :depth], p, preferred_element_type=jnp.float32)
        token = lax.broadcasted_iota(jnp.int32, (1, ROWS), 1) % TOKENS + j * TOKENS
        factor = jnp.where(token < length, 1.0 / jnp.sum(total, axis=0, keepdims=True), 0.0)
        out = (acc * factor).T.astype(jnp.bfloat16)
        for h in range(HALF):
            o_ref[j * TOKENS : (j + 1) * TOKENS, columns(g, hh, h)] = out[h * TOKENS : (h + 1) * TOKENS]

    scores(0, 0, 0)

    def head(g, carry):
        for t in range(6):
            if t < 5:
                scores(g, t + 1, (t + 1) % 2)
            else:
                scores(jnp.minimum(g + 1, HEADS_KV - 1), 0, 0)
            values(g, t, t % 2)
        return carry

    lax.fori_loop(0, HEADS_KV, head, 0)


def body(queries, own_keys, own_values, key_codes, value_codes, code_scales, lengths):
    factors = code_scales.astype(jnp.float32)
    keys = (key_codes.astype(jnp.float32) * factors[:, :, 0]).astype(jnp.bfloat16)
    values = (value_codes.astype(jnp.float32) * factors[:, :, 1]).astype(jnp.bfloat16)
    shard = jnp.concatenate([keys, values.T], axis=0)
    prompt = lax.all_gather(shard[None], "blk", axis=0, tiled=True)
    prompt = lax.all_gather(prompt, "uly", axis=0, tiled=True)
    vmem = pl.BlockSpec(memory_space=pltpu.VMEM)
    out = pl.pallas_call(
        attend,
        out_shape=jax.ShapeDtypeStruct((LENGTH, HEADS_KV * GROUP * D), jnp.bfloat16),
        in_specs=[pl.BlockSpec(memory_space=pltpu.SMEM)] + [vmem] * 4,
        out_specs=vmem,
        scratch_shapes=[
            pltpu.VMEM((2, PROMPT + 256, ROWS), jnp.float32),
            pltpu.VMEM((2, 8, ROWS), jnp.float32),
            pltpu.VMEM((HEADS_KV, D, 256), jnp.bfloat16),
            pltpu.VMEM((TOKENS, ROWS), jnp.float32),
        ],
        compiler_params=pltpu.CompilerParams(vmem_limit_bytes=60 * 2**20),
        cost_estimate=pl.CostEstimate(flops=14_000_000_000, bytes_accessed=16_000_000, transcendentals=27_000_000),
    )(lengths, queries[0], prompt, own_keys[0], own_values[0])
    return out[None]


def solution(mesh):
    placed = (
        P(("blk", "uly"), None, None),
        P(("blk", "uly"), None, None),
        P(("blk", "uly"), None, None),
        P("blk", "uly"),
        P("blk", "uly"),
        P("blk", "uly", None),
        P(("blk", "uly")),
    )
    return jax.shard_map(
        body, mesh=mesh, in_specs=placed, out_specs=P(("blk", "uly"), None, None), check_vma=False
    )
```

time: 476 us -> 271 us (0.57)
  waiting for transfers between devices: 44.5 us -> 214 us
  matrix products: 102 us -> 0 us
  other arithmetic: 98.8 us -> 2.15 us
  local copies, waits for them, and re-layouts: 97.6 us -> 3.12 us
  blocking collectives: 93.2 us -> 0 us
  Pallas kernels: 0 us -> 33.4 us
  starting transfers between devices: 29.9 us -> 0.04 us
  between operations: 1.1 us -> 14.1 us
    all_gather x0 -> x2, waiting for transfers between devices: none -> 214 us  [the longest x1 167 us: body(): prompt = lax.all_gather(prompt, 'uly', axis=0, tiled=True)]
    dot_general x6 -> x0, matrix products: 102 us -> none  [the longest x2 42.9 us: prompt_step(): jnp.einsum('rtkgd,nkd->rkgtn', grouped, prompt_keys, preferred_element_ty...]
    all_gather x3 -> x0, blocking collectives: 93.2 us -> none  [the longest x1 44.6 us: fold_call(): lax.all_gather(code_scales, 'blk', axis=0, tiled=True)]
    unnamed x38 -> x1, local copies, waits for them, and re-layouts: 63 us -> 0.86 us
    unnamed x6 -> x0, other arithmetic: 55.4 us -> none
    all_to_all x4 -> x0, waiting for transfers between devices: 44.5 us -> none  [the longest x1 44.5 us: body(): lax.all_to_all(ordered, 'uly', split_axis=0, concat_axis=2, tiled=True)]
    reduce_sum x3 -> x0, other arithmetic: 40.7 us -> none  [fold_scores(): totals = totals * shrink + jnp.sum(weights, axis=-1)]
    pallas_call x0 -> x1, Pallas kernels: none -> 33.4 us  [body(): pl.pallas_call(attend, out_shape=jax.ShapeDtypeStruct((LENGTH, HEADS_KV *...]
  transfers between devices with their start and end apart: 4 -> 2, of which waited for: 1 -> 2; matrix products, arithmetic and copies ran while one was open for 21% -> 0% of each run, Pallas kernels for 0% -> 0%
where the time goes in v1:
time: 271 us; the launch traced here: 267 us
  waiting for transfers between devices  214 us (79%)
  Pallas kernels  33.4 us (12%)
  between operations  14.1 us (5%)
  local copies, waits for them, and re-layouts  3.12 us (1%)
    all_gather x1, waiting for transfers between devices, body(): prompt = lax.all_gather(prompt, 'uly', axis=0, tiled=True)  167 us
    all_gather x1, waiting for transfers between devices, body(): prompt = lax.all_gather(shard[None], 'blk', axis=0, tiled=True)  46.7 us
    pallas_call x1, Pallas kernels, body(): pl.pallas_call(attend, out_shape=jax.ShapeDtypeStruct((LENGTH, HEADS_KV *...  33.4 us
  transfers between devices with their start and end apart: 2, of which 2 were waited for; matrix products, arithmetic and copies ran while one was open for 0% of the time, Pallas kernels for 0%

profile of v1, /device:TPU:1, one launch (start us, length us, event | category | flops | bytes accessed | tf_op | source)
XLA Modules:
  0.0 266.8 jit_solution(594449466173119258)
XLA Ops:
  6.5 0.0 all-gather.6.cloned.1.call-start
  6.5 0.7 convert_element_type.16
  7.2 0.9 copy.10
  8.1 0.8 fusion
  8.9 0.6 pad_maximum_fusion
  9.6 0.0 all-gather.6.cloned.1.call-update
  9.6 0.0 all-gather.4.cloned.1.call-start
  9.7 46.7 %all-gather.6.cloned.1.call-done = bf16[4096,128]{0,1:T(8,128)(2,1)} async-done(((bf16[256,128]{0,1:T(8,128)(2,1)}), bf16[4096,128]{0,1:T(8,128)(2,1)}) %all-gather.6.cloned.1.call-update) | async-done | bytes 1048592 | tf_op jit(solution)/shard_map/all_gather | solution.py:107
  56.3 2.3 copy.11
  58.6 0.0 all-gather.4.cloned.1.call-update
  59.2 167.3 %all-gather.4.cloned.1.call-done.kv_ref = bf16[128,256,128]{2,1,0:T(8,128)(2,1)} async-done(((bf16[16,256,128]{2,1,0:T(8,128)(2,1)}), bf16[128,256,128]{2,1,0:T(8,128)(2,1)}) %all-gather.4.cloned.1.call-update) | async-done | bytes 8388624 | tf_op jit(solution)/shard_map/all_gather | solution.py:108
  226.6 33.4 %shard_map.73 = bf16[192,8192]{1,0:T(8,128)(2,1)} custom-call(s32[1]{0:T(128)S(6)} %copy.12.lengths_ref, bf16[192,8192]{1,0:T(8,128)(2,1)} %bitcast.12, bf16[128,256,128]{2,1,0:T(8,128)(2,1)} %all-gather.4.cloned.1.call-done.kv_ref, bf16[192,1024]{1,0:T(8,128)(2,1)} %bitcast.13, bf16[192,1024]{1,0:T(8,128)(2,1)} %bitcast.14), custom_call_target="tpu_custom_call" | custom-call | flops 14000000000 | bytes 16000000 | tf_op jit(solution)/shard_map/pallas_call | solution.py:110
  (2 shorter events, 0.0 us)
Async XLA Ops:
  6.5 49.8 %all-gather.6.cloned.1.call-start = ((), (), s32[]{:S(2)}) async-start(), calls=%async_computation.1 | async-start | bytes 1114112 | tf_op jit(solution)/shard_map/all_gather | solution.py:107
  9.6 217.0 %all-gather.4.cloned.1.call-start = ((), (), s32[]{:S(2)}) async-start(), calls=%async_computation | async-start | bytes 9437184 | tf_op jit(solution)/shard_map/all_gather | solution.py:108
Sparse Core Ops, SparseCore 0:
  9.7 46.5 all-gather.5
  58.7 167.7 all-gather.3

commit v2 on v1

v2 whole, which is shorter than its diff:
```python
import math

import jax
import jax.numpy as jnp
from jax import lax
from jax.experimental import pallas as pl
from jax.experimental.pallas import tpu as pltpu
from jax.sharding import PartitionSpec as P

MESH = pl.DeviceIdType.MESH
D = 128
HEADS_KV = 8
GROUP = 8
LENGTH = 192
CHUNK = 512
PROMPT = 2048
TOKENS = 64
HALF = 4
ROWS = HALF * TOKENS
TILES = 6
SCALE = math.log2(math.e) / math.sqrt(D)
STEPS = (2, 1, 3)


def dot_t(a, b):
    return lax.dot_general(a, b, (((1,), (1,)), ((), ())), preferred_element_type=jnp.float32)


def attend(
    scales_ref, kc_ref, vc_ref, lengths_ref, q_hbm, ok_hbm, ov_hbm, out_hbm,
    q_ref, ok_ref, ov_ref, o_ref, kbuf, vbuf, s_ref, m_ref, ovt_ref, mask_ref, acc_ref, state_ref,
    in_sem, out_sem, x_send, x_recv, k1_send, k1_recv, v1_send, v1_recv,
    k2_send, k2_recv, v2_send, v2_recv, sk_send, sk_recv, sv_send, sv_recv,
):
    blk = lax.axis_index("blk")
    uly = lax.axis_index("uly")
    x, yl = uly // 2, uly % 2
    z, yh, core = blk // 4, (blk // 2) % 2, blk % 2
    y = yh * 2 + yl
    other = 1 - core

    def device(xx, yy, zz, cc):
        return (zz * 4 + (yy // 2) * 2 + cc, xx * 2 + yy % 2)

    def along_x(d):
        return device((x + d) % 4, y, z, core)

    def along_y(d):
        return device(x, (y + d) % 4, z, core)

    def along_z(d):
        return device(x, y, (z + d) % 4, core)

    sibling = device(x, y, z, other)

    def plane(p):
        return (x + p + p // 2 - 2 * (p // 3)) % 4

    barrier = pltpu.get_barrier_semaphore()
    for d in STEPS:
        for to in (along_x(d), along_y(d), along_z(d)):
            pl.semaphore_signal(barrier, inc=1, device_id=to, device_id_type=MESH)
    pl.semaphore_signal(barrier, inc=1, device_id=sibling, device_id_type=MESH)

    loads = [
        pltpu.make_async_copy(a, b, in_sem.at[i])
        for i, (a, b) in enumerate(((ok_hbm, ok_ref), (ov_hbm, ov_ref), (q_hbm, q_ref)))
    ]
    for load in loads:
        load.start()

    factors = scales_ref[...].astype(jnp.float32)
    turned = kc_ref[...].astype(jnp.float32).T * factors[0:1]
    kbuf[x, yl, core, z, yh] = turned.T.astype(jnp.bfloat16)
    turned = vc_ref[...].astype(jnp.float32).T * factors[1:2]
    vbuf[x, yl, core, yh, z] = turned.astype(jnp.bfloat16)

    pl.semaphore_wait(barrier, 10)

    def move(ref, send, recv, to):
        return pltpu.make_async_remote_copy(
            src_ref=ref, dst_ref=ref, send_sem=send, recv_sem=recv, device_id=to, device_id_type=MESH
        )

    def x_moves(i):
        d = (1, 3, 2)[i]
        back = (4 - d) % 4
        out = [
            move(kbuf.at[x, yl, core, z, yh], x_send.at[i, 0], x_recv.at[i, 0], along_x(back)),
            move(vbuf.at[x, yl, core, yh, z], x_send.at[i, 1], x_recv.at[i, 1], along_x(back)),
        ]
        return out

    def x_arrival(p):
        xp = plane(p)
        return [
            move(kbuf.at[xp, yl, core, z, yh], x_send.at[p - 1, 0], x_recv.at[p - 1, 0], sibling),
            move(vbuf.at[xp, yl, core, yh, z], x_send.at[p - 1, 1], x_recv.at[p - 1, 1], sibling),
        ]

    def first_out(p):
        xp = plane(p)
        out = []
        for i, d in enumerate(STEPS):
            out.append(move(kbuf.at[xp, yl, core, z, yh], k1_send.at[p, i], k1_recv.at[p, i], along_y(d)))
            out.append(move(vbuf.at[xp, yl, core, yh, z], v1_send.at[p, i], v1_recv.at[p, i], along_z(d)))
        return out

    def k1_in(p, i):
        xp = plane(p)
        ys = (y + 4 - STEPS[i]) % 4
        return move(kbuf.at[xp, ys % 2, core, z, ys // 2], k1_send.at[p, i], k1_recv.at[p, i], sibling)

    def v1_in(p, i):
        xp = plane(p)
        zs = (z + 4 - STEPS[i]) % 4
        return move(vbuf.at[xp, yl, core, yh, zs], v1_send.at[p, i], v1_recv.at[p, i], sibling)

    def head(a):
        return yl if a == 0 else 1 - yl

    def k2_out(p, a, i):
        xp = plane(p)
        return move(kbuf.at[xp, head(a), core, z], k2_send.at[p, a, i], k2_recv.at[p, a, i], along_z(STEPS[i]))

    def k2_in(p, a, i):
        xp = plane(p)
        zs = (z + 4 - STEPS[i]) % 4
        return move(kbuf.at[xp, head(a), core, zs], k2_send.at[p, a, i], k2_recv.at[p, a, i], sibling)

    def v2_out(p, i):
        xp = plane(p)
        return move(vbuf.at[xp, yl, core, yh], v2_send.at[p, i], v2_recv.at[p, i], along_y(STEPS[i]))

    def v2_in(p, i):
        xp = plane(p)
        ys = (y + 4 - STEPS[i]) % 4
        return move(vbuf.at[xp, ys % 2, core, ys // 2], v2_send.at[p, i], v2_recv.at[p, i], sibling)

    def sk_out(p, a, i):
        xp = plane(p)
        zs = z if i == 3 else (z + 4 - STEPS[i]) % 4
        return move(kbuf.at[xp, head(a), core, zs], sk_send.at[p, a, i], sk_recv.at[p, a, i], sibling)

    def sk_in(p, a, i):
        xp = plane(p)
        zs = z if i == 3 else (z + 4 - STEPS[i]) % 4
        return move(kbuf.at[xp, head(a), other, zs], sk_send.at[p, a, i], sk_recv.at[p, a, i], sibling)

    def sv_out(p, i):
        xp = plane(p)
        ys = y if i == 3 else (y + 4 - STEPS[i]) % 4
        return move(vbuf.at[xp, ys % 2, core, ys // 2], sv_send.at[p, i], sv_recv.at[p, i], sibling)

    def sv_in(p, i):
        xp = plane(p)
        ys = y if i == 3 else (y + 4 - STEPS[i]) % 4
        return move(vbuf.at[xp, ys % 2, other, ys // 2], sv_send.at[p, i], sv_recv.at[p, i], sibling)

    def start_first(p):
        for c in first_out(p):
            c.start()

    def start_second(p):
        k1_in(p, 0).wait_recv()
        for i in range(3):
            k2_out(p, 0, i).start()
        sk_out(p, 0, 3).start()
        for i in range(3):
            v1_in(p, i).wait_recv()
        for i in range(3):
            v2_out(p, i).start()
        sv_out(p, 3).start()
        for i in (1, 2):
            k1_in(p, i).wait_recv()
        for i in range(3):
            k2_out(p, 1, i).start()
        sk_out(p, 1, 3).start()

    def share_own(p):
        for i in (1, 2, 0):
            k2_in(p, 0, i).wait_recv()
            sk_out(p, 0, i).start()
        v2_in(p, 0).wait_recv()
        sv_out(p, 0).start()

    def share_other(p):
        for i in (1, 2, 0):
            k2_in(p, 1, i).wait_recv()
            sk_out(p, 1, i).start()
        for i in (1, 2):
            v2_in(p, i).wait_recv()
            sv_out(p, i).start()

    def have_own(p):
        for i in range(4):
            sk_in(p, 0, i).wait_recv()
        for i in (0, 3):
            sv_in(p, i).wait_recv()

    def have_other(p):
        for i in range(4):
            sk_in(p, 1, i).wait_recv()
        for i in (1, 2):
            sv_in(p, i).wait_recv()

    start_first(0)
    for i in range(3):
        for c in x_moves(i):
            c.start()

    key_at = lax.broadcasted_iota(jnp.int32, (TOKENS, ROWS), 0)
    token_at = lax.broadcasted_iota(jnp.int32, (TOKENS, ROWS), 1) % TOKENS
    mask_ref[...] = jnp.where(token_at >= key_at, 0.0, -jnp.inf).astype(jnp.float32)
    length = lengths_ref[0]

    def columns(g, hh, h):
        return pl.ds(pl.multiple_of((g * GROUP + hh * HALF + h) * D, D), D)

    def queries(g, t):
        hh, j = t // 3, t % 3
        q = jnp.concatenate([q_ref[j * TOKENS : (j + 1) * TOKENS, columns(g, hh, h)] for h in range(HALF)], axis=0)
        q = q.astype(jnp.float32) * SCALE
        high = q.astype(jnp.bfloat16)
        low = (q - high.astype(jnp.float32)).astype(jnp.bfloat16)
        return jnp.concatenate([high, low], axis=1)

    def own_part(g, t):
        j = t % 3
        n = (j + 1) * TOKENS
        keys = ok_ref[:n, pl.ds(pl.multiple_of(g * D, D), D)]
        s = dot_t(jnp.concatenate([keys, keys], axis=1), queries(g, t))
        last = s[j * TOKENS :] + mask_ref[...]
        s = jnp.concatenate([s[: j * TOKENS], last], axis=0) if j else last
        top = jnp.max(s, axis=0, keepdims=True)
        p = jnp.exp2(s - top)
        total = jnp.sum(p.reshape(n // 8, 8, ROWS), axis=0)
        depth = 128 if j < 2 else 256
        p = p.astype(jnp.bfloat16)
        if depth > n:
            p = jnp.concatenate([p, jnp.zeros((depth - n, ROWS), jnp.bfloat16)], axis=0)
        acc_ref[g * TILES + t] = jnp.dot(ovt_ref[g, :, :depth], p, preferred_element_type=jnp.float32)
        state_ref[g * TILES + t, 0] = jnp.broadcast_to(top, (8, ROWS))
        state_ref[g * TILES + t, 1] = total

    def own_head(g, carry):
        cols = pl.ds(pl.multiple_of(g * D, D), D)
        ovt_ref[g] = jnp.concatenate([ov_ref[:, cols].T, jnp.zeros((D, 256 - LENGTH), jnp.bfloat16)], axis=1)
        for t in range(TILES):
            own_part(g, t)
        return carry

    def key_blocks(xp, hd):
        return [kbuf[xp, hd, c, zz, hh] for c in range(2) for zz in range(4) for hh in range(2)]

    def value_blocks(xp, hd):
        return [vbuf[xp, hd, c, hh, zz] for c in range(2) for zz in range(4) for hh in range(2)]

    per = CHUNK // D

    def scores(p, a, t, slot):
        xp, hd = plane(p), head(a)
        g = xp * 2 + hd
        q = queries(g, t)
        blocks = key_blocks(xp, hd)
        top = state_ref[g * TILES + t, 0]
        for c in range(PROMPT // CHUNK):
            keys = jnp.concatenate(blocks[c * per : (c + 1) * per], axis=0)
            s = dot_t(jnp.concatenate([keys, keys], axis=1), q)
            s_ref[slot, c * CHUNK : (c + 1) * CHUNK] = s
            top = jnp.maximum(top, jnp.max(s.reshape(CHUNK // 8, 8, ROWS), axis=0))
        m_ref[slot] = jnp.broadcast_to(jnp.max(top, axis=0, keepdims=True), (8, ROWS))

    def values(p, a, t, slot):
        xp, hd = plane(p), head(a)
        g = xp * 2 + hd
        hh, j = t // 3, t % 3
        blocks = value_blocks(xp, hd)
        top = m_ref[slot]
        shrink = jnp.exp2(state_ref[g * TILES + t, 0] - top)
        total = state_ref[g * TILES + t, 1] * shrink
        acc = acc_ref[g * TILES + t] * shrink[:1]
        for c in range(PROMPT // CHUNK):
            w = jnp.exp2(s_ref[slot, c * CHUNK : (c + 1) * CHUNK] - top[:1])
            total = total + jnp.sum(w.reshape(CHUNK // 8, 8, ROWS), axis=0)
            turned = jnp.concatenate(blocks[c * per : (c + 1) * per], axis=1)
            acc = acc + jnp.dot(turned, w.astype(jnp.bfloat16), preferred_element_type=jnp.float32)
        token = lax.broadcasted_iota(jnp.int32, (1, ROWS), 1) % TOKENS + j * TOKENS
        factor = jnp.where(token < length, 1.0 / jnp.sum(total, axis=0, keepdims=True), 0.0)
        out = (acc * factor).T.astype(jnp.bfloat16)
        for h in range(HALF):
            o_ref[j * TOKENS : (j + 1) * TOKENS, columns(g, hh, h)] = out[h * TOKENS : (h + 1) * TOKENS]

    def out_copy(p, a):
        g = plane(p) * 2 + head(a)
        cols = pl.ds(pl.multiple_of(g * GROUP * D, GROUP * D), GROUP * D)
        return pltpu.make_async_copy(o_ref.at[:, cols], out_hbm.at[:, cols], out_sem.at[p, a])

    for load in loads:
        load.wait()
    lax.fori_loop(0, 4, own_head, 0)
    start_second(0)
    lax.fori_loop(4, HEADS_KV, own_head, 0)
    share_own(0)
    for c in x_arrival(1):
        c.wait_recv()
    start_first(1)
    have_own(0)
    scores(0, 0, 0, 0)

    def work(p, final):
        for u in range(2 * TILES):
            a, t = u // TILES, u % TILES
            if u == 2:
                share_other(p)
            if u == 3 and not final:
                start_second(p + 1)
            if u == 5:
                have_other(p)
            if u == 8 and not final:
                share_own(p + 1)
            if u == 9 and not final:
                @pl.when(p < 2)
                def _():
                    for c in x_arrival(p + 2):
                        c.wait_recv()
                    start_first(p + 2)
            if u == 11 and not final:
                have_own(p + 1)
            if u < 11:
                scores(p, (u + 1) // TILES, (u + 1) % TILES, (u + 1) % 2)
            elif not final:
                scores(p + 1, 0, 0, 0)
            values(p, a, t, u % 2)
            if t == TILES - 1:
                out_copy(p, a).start()

    def planes(p, carry):
        work(p, False)
        return carry

    lax.fori_loop(0, 3, planes, 0)
    work(3, True)

    for i in range(3):
        for c in x_moves(i):
            c.wait_send()

    def settle(p, carry):
        for c in first_out(p):
            c.wait_send()
        for i in range(3):
            for a in range(2):
                k2_out(p, a, i).wait_send()
            v2_out(p, i).wait_send()
        for i in range(4):
            for a in range(2):
                sk_out(p, a, i).wait_send()
            sv_out(p, i).wait_send()
        for a in range(2):
            out_copy(p, a).wait()
        return carry

    lax.fori_loop(0, 4, settle, 0)


def body(queries, own_keys, own_values, key_codes, value_codes, code_scales, lengths):
    scales = jnp.transpose(code_scales[:, 0, :])
    vmem = pl.BlockSpec(memory_space=pltpu.VMEM)
    hbm = pl.BlockSpec(memory_space=pl.ANY)
    dma = pltpu.SemaphoreType.DMA
    width = HEADS_KV * GROUP * D
    out = pl.pallas_call(
        attend,
        out_shape=jax.ShapeDtypeStruct((LENGTH, width), jnp.bfloat16),
        in_specs=[vmem, vmem, vmem, pl.BlockSpec(memory_space=pltpu.SMEM), hbm, hbm, hbm],
        out_specs=hbm,
        scratch_shapes=[
            pltpu.VMEM((LENGTH, width), jnp.bfloat16),
            pltpu.VMEM((LENGTH, HEADS_KV * D), jnp.bfloat16),
            pltpu.VMEM((LENGTH, HEADS_KV * D), jnp.bfloat16),
            pltpu.VMEM((LENGTH, width), jnp.bfloat16),
            pltpu.VMEM((4, 2, 2, 4, 2, D, D), jnp.bfloat16),
            pltpu.VMEM((4, 2, 2, 2, 4, D, D), jnp.bfloat16),
            pltpu.VMEM((2, PROMPT, ROWS), jnp.float32),
            pltpu.VMEM((2, 8, ROWS), jnp.float32),
            pltpu.VMEM((HEADS_KV, D, 256), jnp.bfloat16),
            pltpu.VMEM((TOKENS, ROWS), jnp.float32),
            pltpu.VMEM((HEADS_KV * TILES, D, ROWS), jnp.float32),
            pltpu.VMEM((HEADS_KV * TILES, 2, 8, ROWS), jnp.float32),
            dma((3,)), dma((4, 2)),
            dma((3, 2)), dma((3, 2)),
            dma((4, 3)), dma((4, 3)),
            dma((4, 3)), dma((4, 3)),
            dma((4, 2, 3)), dma((4, 2, 3)),
            dma((4, 3)), dma((4, 3)),
            dma((4, 2, 4)), dma((4, 2, 4)),
            dma((4, 4)), dma((4, 4)),
        ],
        compiler_params=pltpu.CompilerParams(
            collective_id=0, has_side_effects=True, vmem_limit_bytes=56 * 2**20
        ),
        cost_estimate=pl.CostEstimate(flops=14_000_000_000, bytes_accessed=8_000_000, transcendentals=27_000_000),
    )(scales, key_codes, value_codes, lengths, queries[0], own_keys[0], own_values[0])
    return out[None]


def solution(mesh):
    placed = (
        P(("blk", "uly"), None, None),
        P(("blk", "uly"), None, None),
        P(("blk", "uly"), None, None),
        P("blk", "uly"),
        P("blk", "uly"),
        P("blk", "uly", None),
        P(("blk", "uly")),
    )
    return jax.shard_map(
        body, mesh=mesh, in_specs=placed, out_specs=P(("blk", "uly"), None, None), check_vma=False
    )
```

time: 271 us -> 72.8 us (0.27); the launches traced: 267 us -> 72.6 us
  waiting for transfers between devices: 214 us -> 0 us
  Pallas kernels: 33.4 us -> 68.1 us
  between operations: 14.1 us -> 0.66 us
    all_gather x2 -> x0, waiting for transfers between devices: 214 us -> none  [the longest x1 167 us: body(): prompt = lax.all_gather(prompt, 'uly', axis=0, tiled=True)]
    pallas_call x1, Pallas kernels: 33.4 us -> 68.1 us  [body(): pl.pallas_call(attend, out_shape=jax.ShapeDtypeStruct((LENGTH, width), jn...]
    unnamed x1, local copies, waits for them, and re-layouts: 0.86 us -> 3.86 us
  transfers between devices with their start and end apart: 2 -> 0, of which waited for: 2 -> 0; matrix products, arithmetic and copies ran while one was open for 0% -> 0% of each run, Pallas kernels for 0% -> 0%
where the time goes in v2:
time: 72.8 us; the launch traced here: 72.6 us
  Pallas kernels  68.1 us (94%)
  local copies, waits for them, and re-layouts  3.86 us (5%)
    pallas_call x1, Pallas kernels, body(): pl.pallas_call(attend, out_shape=jax.ShapeDtypeStruct((LENGTH, width), jn...  68.1 us
    unnamed x1, local copies, waits for them, and re-layouts  3.86 us

profile of v2, /device:TPU:1, one launch (start us, length us, event | category | flops | bytes accessed | tf_op | source)
XLA Modules:
  0.0 72.6 jit_solution(17816468499119861958)
XLA Ops:
  0.7 68.1 %shard_map.73 = bf16[192,8192]{1,0:T(8,128)(2,1)} custom-call(bf16[2,128]{1,0:T(2,128)(2,1)} %bitcast.11, bf16[128,128]{1,0:T(8,128)(2,1)} %kc_ref.1, bf16[128,128]{1,0:T(8,128)(2,1)} %vc_ref.1, s32[1]{0:T(128)S(6)} %copy.9.lengths_ref, bf16[192,8192]{1,0:T(8,128)(2,1)} %bitcast.8, bf16[192,1024]{1,0:T(8,128)(2,1)} %bitcast.9, bf16[192,1024]{1,0:T(8,128)(2,1)} %bitcast.10), custom_call_target="tpu_custom_call" | custom-call | flops 14000000000 | bytes 8000000 | tf_op jit(solution)/shard_map/pallas_call | solution.py:373
  68.8 3.9 %copy.10 = bf16[1,192,8192]{2,1,0:T(8,128)(2,1)} copy(bf16[1,192,8192]{2,1,0:T(8,128)(2,1)} %bitcast.7) | data formatting | bytes 6291456

commit v3 on v2

v3 whole, which is shorter than its diff:
```python
import math

import jax
import jax.numpy as jnp
from jax import lax
from jax.experimental import pallas as pl
from jax.experimental.pallas import tpu as pltpu
from jax.sharding import PartitionSpec as P

MESH = pl.DeviceIdType.MESH
D = 128
HEADS_KV = 8
GROUP = 8
LENGTH = 192
CHUNK = 512
PROMPT = 2048
TOKENS = 64
HALF = 4
ROWS = HALF * TOKENS
TILES = 6
SCALE = math.log2(math.e) / math.sqrt(D)
STEPS = (2, 1, 3)
NEAR = 96


def dot_t(a, b):
    return lax.dot_general(a, b, (((1,), (1,)), ((), ())), preferred_element_type=jnp.float32)


def attend(
    scales_hbm, kc_hbm, vc_hbm, lengths_ref, q_hbm, ok_hbm, ov_hbm, o_ref,
    kc_ref, vc_ref, scales_ref, q_ref, ok_ref, ov_ref, kbuf, vbuf, s_ref, m_ref, mask_ref, acc_ref, state_ref,
    in_sem, x_send, x_recv, far_send, far_recv, k1_send, k1_recv, v1_send, v1_recv,
    k2_send, k2_recv, v2_send, v2_recv, sk_send, sk_recv, sv_send, sv_recv, share_send, share_recv,
):
    blk = lax.axis_index("blk")
    uly = lax.axis_index("uly")
    x, yl = uly // 2, uly % 2
    z, yh, core = blk // 4, (blk // 2) % 2, blk % 2
    y = yh * 2 + yl
    other = 1 - core

    def device(xx, yy, zz, cc):
        return (zz * 4 + (yy // 2) * 2 + cc, xx * 2 + yy % 2)

    def along_x(d):
        return device((x + d) % 4, y, z, core)

    def along_y(d):
        return device(x, (y + d) % 4, z, core)

    def along_z(d):
        return device(x, y, (z + d) % 4, core)

    sibling = device(x, y, z, other)

    def plane(p):
        return (x + p + p // 2 - 2 * (p // 3)) % 4

    barrier = pltpu.get_barrier_semaphore()
    for d in STEPS:
        for to in (along_x(d), along_y(d), along_z(d)):
            pl.semaphore_signal(barrier, inc=1, device_id=to, device_id_type=MESH)
    pl.semaphore_signal(barrier, inc=1, device_id=sibling, device_id_type=MESH)

    loads = [
        pltpu.make_async_copy(a, b, in_sem.at[i])
        for i, (a, b) in enumerate(
            (
                (scales_hbm, scales_ref), (kc_hbm, kc_ref), (vc_hbm, vc_ref),
                (ok_hbm, ok_ref), (ov_hbm, ov_ref), (q_hbm, q_ref),
            )
        )
    ]
    for load in loads:
        load.start()
    for load in loads[:3]:
        load.wait()

    factors = scales_ref[...].astype(jnp.float32)
    turned = kc_ref[...].astype(jnp.float32).T * factors[0:1]
    kbuf[x, yl, core, z, yh] = turned.T.astype(jnp.bfloat16)
    turned = vc_ref[...].astype(jnp.float32).T * factors[1:2]
    vbuf[x, yl, core, yh, z] = turned.astype(jnp.bfloat16)

    pl.semaphore_wait(barrier, 10)

    def move(ref, send, recv, to):
        return pltpu.make_async_remote_copy(
            src_ref=ref, dst_ref=ref, send_sem=send, recv_sem=recv, device_id=to, device_id_type=MESH
        )

    def rows(p):
        return pl.ds(0, D if isinstance(p, int) and p == 0 else NEAR)

    far = pl.ds(NEAR, D - NEAR)

    def head(a):
        return yl if a == 0 else 1 - yl

    def y_of(i):
        return (y + 4 - STEPS[i]) % 4

    def z_of(i):
        return (z + 4 - STEPS[i]) % 4

    def x_out(i):
        to = along_x((3, 1, 2)[i])
        return [
            move(kbuf.at[x, yl, core, z, yh, pl.ds(0, NEAR)], x_send.at[i, 0], x_recv.at[i, 0], to),
            move(vbuf.at[x, yl, core, yh, z, pl.ds(0, NEAR)], x_send.at[i, 1], x_recv.at[i, 1], to),
        ]

    def x_in(p):
        xp = plane(p)
        return [
            move(kbuf.at[xp, yl, core, z, yh, pl.ds(0, NEAR)], x_send.at[p - 1, 0], x_recv.at[p - 1, 0], sibling),
            move(vbuf.at[xp, yl, core, yh, z, pl.ds(0, NEAR)], x_send.at[p - 1, 1], x_recv.at[p - 1, 1], sibling),
        ]

    def far_out(i, a):
        to = along_x((3, 1, 2)[i])
        return [
            move(kbuf.at[x, head(a), core, :, :, far], far_send.at[i, a, 0], far_recv.at[i, a, 0], to),
            move(vbuf.at[x, head(a), core, :, :, far], far_send.at[i, a, 1], far_recv.at[i, a, 1], to),
        ]

    def far_in(p, a):
        xp = plane(p)
        return [
            move(kbuf.at[xp, head(a), core, :, :, far], far_send.at[p - 1, a, 0], far_recv.at[p - 1, a, 0], sibling),
            move(vbuf.at[xp, head(a), core, :, :, far], far_send.at[p - 1, a, 1], far_recv.at[p - 1, a, 1], sibling),
        ]

    def first_out(p):
        xp = plane(p)
        out = []
        for i, d in enumerate(STEPS):
            out.append(move(kbuf.at[xp, yl, core, z, yh, rows(p)], k1_send.at[p, i], k1_recv.at[p, i], along_y(d)))
            out.append(move(vbuf.at[xp, yl, core, yh, z, rows(p)], v1_send.at[p, i], v1_recv.at[p, i], along_z(d)))
        return out

    def k1_in(p, i):
        ys = y_of(i)
        return move(kbuf.at[plane(p), ys % 2, core, z, ys // 2, rows(p)], k1_send.at[p, i], k1_recv.at[p, i], sibling)

    def v1_in(p, i):
        return move(vbuf.at[plane(p), yl, core, yh, z_of(i), rows(p)], v1_send.at[p, i], v1_recv.at[p, i], sibling)

    def k2_out(p, a, i):
        return move(kbuf.at[plane(p), head(a), core, z, :, rows(p)], k2_send.at[p, a, i], k2_recv.at[p, a, i], along_z(STEPS[i]))

    def k2_in(p, a, i):
        return move(kbuf.at[plane(p), head(a), core, z_of(i), :, rows(p)], k2_send.at[p, a, i], k2_recv.at[p, a, i], sibling)

    def v2_out(p, i):
        return move(vbuf.at[plane(p), yl, core, yh, :, rows(p)], v2_send.at[p, i], v2_recv.at[p, i], along_y(STEPS[i]))

    def v2_in(p, i):
        ys = y_of(i)
        return move(vbuf.at[plane(p), ys % 2, core, ys // 2, :, rows(p)], v2_send.at[p, i], v2_recv.at[p, i], sibling)

    def sk(a, i, c):
        return move(kbuf.at[x, head(a), c, z if i == 3 else z_of(i)], sk_send.at[a, i], sk_recv.at[a, i], sibling)

    def sv(i, c):
        ys = y if i == 3 else y_of(i)
        return move(vbuf.at[x, ys % 2, c, ys // 2], sv_send.at[i], sv_recv.at[i], sibling)

    def share(p, a, c):
        xp = plane(p)
        return [
            move(kbuf.at[xp, head(a), c], share_send.at[p - 1, a, 0], share_recv.at[p - 1, a, 0], sibling),
            move(vbuf.at[xp, head(a), c], share_send.at[p - 1, a, 1], share_recv.at[p - 1, a, 1], sibling),
        ]

    def start(copies):
        for c in copies:
            c.start()

    def arrive(copies):
        for c in copies:
            c.wait_recv()

    def start_first(p):
        if not (isinstance(p, int) and p == 0):
            arrive(x_in(p))
        start(first_out(p))

    def second_own(p):
        near = isinstance(p, int) and p == 0
        k1_in(p, 0).wait_recv()
        start([k2_out(p, 0, i) for i in range(3)])
        if near:
            sk(0, 3, core).start()
        arrive([v1_in(p, i) for i in range(3)])
        v2_out(p, 0).start()
        if near:
            sv(3, core).start()
        arrive([k1_in(p, i) for i in (1, 2)])
        if near:
            sk(1, 3, core).start()

    def second_other(p):
        start([k2_out(p, 1, i) for i in range(3)])
        start([v2_out(p, i) for i in (1, 2)])

    def start_second(p):
        second_own(p)
        second_other(p)

    def share_first(a):
        for i in (1, 2, 0):
            k2_in(0, a, i).wait_recv()
            sk(a, i, core).start()
        for i in ((0,), (1, 2))[a]:
            v2_in(0, i).wait_recv()
            sv(i, core).start()
        for i in range(3):
            start(far_out(i, a))

    def have_first(a):
        arrive([sk(a, i, other) for i in range(4)])
        arrive([sv(i, other) for i in ((0, 3), (1, 2))[a]])

    def share_later(p, a):
        arrive([k2_in(p, a, i) for i in (1, 2, 0)])
        kf, vf = far_in(p, a)
        kf.wait_recv()
        ks, vs = share(p, a, core)
        ks.start()
        arrive([v2_in(p, i) for i in ((0,), (1, 2))[a]])
        vf.wait_recv()
        vs.start()

    def have_later(p, a):
        arrive(share(p, a, other))

    start_first(0)
    for i in range(3):
        start(x_out(i))

    key_at = lax.broadcasted_iota(jnp.int32, (TOKENS, ROWS), 0)
    token_at = lax.broadcasted_iota(jnp.int32, (TOKENS, ROWS), 1) % TOKENS
    mask_ref[...] = jnp.where(token_at >= key_at, 0.0, -jnp.inf).astype(jnp.float32)
    length = lengths_ref[0]

    def columns(g, hh, h):
        return pl.ds(pl.multiple_of((g * GROUP + hh * HALF + h) * D, D), D)

    def queries(g, t):
        hh, j = t // 3, t % 3
        q = jnp.concatenate([q_ref[j * TOKENS : (j + 1) * TOKENS, columns(g, hh, h)] for h in range(HALF)], axis=0)
        q = q.astype(jnp.float32) * SCALE
        high = q.astype(jnp.bfloat16)
        low = (q - high.astype(jnp.float32)).astype(jnp.bfloat16)
        return jnp.concatenate([high, low], axis=1)

    def own_head(g, carry):
        cols = pl.ds(pl.multiple_of(g * D, D), D)
        turned = ov_ref[:, cols].T
        keys = ok_ref[:, cols]
        keys = jnp.concatenate([keys, keys], axis=1)
        mask = mask_ref[...]
        scored = []
        for t in range(TILES):
            j = t % 3
            s = dot_t(keys[: (j + 1) * TOKENS], queries(g, t))
            last = s[j * TOKENS :] + mask
            scored.append(jnp.concatenate([s[: j * TOKENS], last], axis=0) if j else last)
        weighed = []
        for t in range(TILES):
            n = (t % 3 + 1) * TOKENS
            s = scored[t]
            top = jnp.max(s, axis=0, keepdims=True)
            p = jnp.exp2(s - top)
            state_ref[g * TILES + t, 0] = jnp.broadcast_to(top, (8, ROWS))
            state_ref[g * TILES + t, 1] = jnp.sum(p.reshape(n // 8, 8, ROWS), axis=0)
            weighed.append(p.astype(jnp.bfloat16))
        for t in range(TILES):
            n = (t % 3 + 1) * TOKENS
            acc_ref[g * TILES + t] = jnp.dot(turned[:, :n], weighed[t], preferred_element_type=jnp.float32)
        return carry

    def key_blocks(xp, hd):
        return [kbuf[xp, hd, c, zz, hh] for c in range(2) for zz in range(4) for hh in range(2)]

    def value_blocks(xp, hd):
        return [vbuf[xp, hd, c, hh, zz] for c in range(2) for zz in range(4) for hh in range(2)]

    per = CHUNK // D

    def scores(p, a, t, slot):
        xp, hd = plane(p), head(a)
        g = xp * 2 + hd
        q = queries(g, t)
        blocks = key_blocks(xp, hd)
        top = state_ref[g * TILES + t, 0]
        for c in range(PROMPT // CHUNK):
            keys = jnp.concatenate(blocks[c * per : (c + 1) * per], axis=0)
            s = dot_t(jnp.concatenate([keys, keys], axis=1), q)
            s_ref[slot, c * CHUNK : (c + 1) * CHUNK] = s
            top = jnp.maximum(top, jnp.max(s.reshape(CHUNK // 8, 8, ROWS), axis=0))
        m_ref[slot] = jnp.broadcast_to(jnp.max(top, axis=0, keepdims=True), (8, ROWS))

    def values(p, a, t, slot):
        xp, hd = plane(p), head(a)
        g = xp * 2 + hd
        hh, j = t // 3, t % 3
        blocks = value_blocks(xp, hd)
        top = m_ref[slot]
        shrink = jnp.exp2(state_ref[g * TILES + t, 0] - top)
        total = state_ref[g * TILES + t, 1] * shrink
        acc = acc_ref[g * TILES + t] * shrink[:1]
        for c in range(PROMPT // CHUNK):
            w = jnp.exp2(s_ref[slot, c * CHUNK : (c + 1) * CHUNK] - top[:1])
            total = total + jnp.sum(w.reshape(CHUNK // 8, 8, ROWS), axis=0)
            turned = jnp.concatenate(blocks[c * per : (c + 1) * per], axis=1)
            acc = acc + jnp.dot(turned, w.astype(jnp.bfloat16), preferred_element_type=jnp.float32)
        token = lax.broadcasted_iota(jnp.int32, (1, ROWS), 1) % TOKENS + j * TOKENS
        factor = jnp.where(token < length, 1.0 / jnp.sum(total, axis=0, keepdims=True), 0.0)
        out = (acc * factor).T.astype(jnp.bfloat16)
        for h in range(HALF):
            o_ref[j * TOKENS : (j + 1) * TOKENS, columns(g, hh, h)] = out[h * TOKENS : (h + 1) * TOKENS]

    for load in loads[3:]:
        load.wait()
    lax.fori_loop(0, 2, own_head, 0)
    second_own(0)
    start_first(1)
    lax.fori_loop(2, 5, own_head, 0)
    share_first(0)
    second_other(0)
    lax.fori_loop(5, HEADS_KV, own_head, 0)
    second_own(1)
    have_first(0)
    scores(0, 0, 0, 0)

    def work(p, place):
        for u in range(2 * TILES):
            a, t = u // TILES, u % TILES
            if place == 0:
                if u == 0:
                    start_first(2)
                    start_first(3)
                if u == 2:
                    second_other(1)
                if u == 3:
                    share_first(1)
                if u == 5:
                    have_first(1)
                    start_second(2)
                if u == 9:
                    start_second(3)
            else:
                if u == 1:
                    share_later(p, 1)
                if u == 5:
                    have_later(p, 1)
            if place < 2 and u == 7:
                share_later(p + 1, 0)
            if place < 2 and u == 11:
                have_later(p + 1, 0)
            if u < 11:
                scores(p, (u + 1) // TILES, (u + 1) % TILES, (u + 1) % 2)
            elif place < 2:
                scores(p + 1, 0, 0, 0)
            values(p, a, t, u % 2)

    def planes(p, carry):
        work(p, 1)
        return carry

    work(0, 0)
    lax.fori_loop(1, 3, planes, 0)
    work(3, 2)

    def sent(copies):
        for c in copies:
            c.wait_send()

    def settle(p):
        sent(first_out(p))
        for i in range(3):
            sent([k2_out(p, a, i) for a in range(2)])
            v2_out(p, i).wait_send()

    for i in range(3):
        sent(x_out(i))
        for a in range(2):
            sent(far_out(i, a))
    for i in range(4):
        sent([sk(0, i, core), sk(1, i, core), sv(i, core)])
    settle(0)

    def settle_later(p, carry):
        settle(p)
        for a in range(2):
            sent(share(p, a, core))
        return carry

    lax.fori_loop(1, 4, settle_later, 0)


def body(queries, own_keys, own_values, key_codes, value_codes, code_scales, lengths):
    scales = jnp.transpose(code_scales[:, 0, :])
    vmem = pl.BlockSpec(memory_space=pltpu.VMEM)
    hbm = pl.BlockSpec(memory_space=pl.ANY)
    dma = pltpu.SemaphoreType.DMA
    width = HEADS_KV * GROUP * D
    out = pl.pallas_call(
        attend,
        out_shape=pltpu.VMEM((LENGTH, width), jnp.bfloat16),
        in_specs=[hbm, hbm, hbm, pl.BlockSpec(memory_space=pltpu.SMEM), hbm, hbm, hbm],
        out_specs=vmem,
        scratch_shapes=[
            pltpu.VMEM((D, D), jnp.bfloat16),
            pltpu.VMEM((D, D), jnp.bfloat16),
            pltpu.VMEM((2, D), jnp.bfloat16),
            pltpu.VMEM((LENGTH, width), jnp.bfloat16),
            pltpu.VMEM((LENGTH, HEADS_KV * D), jnp.bfloat16),
            pltpu.VMEM((LENGTH, HEADS_KV * D), jnp.bfloat16),
            pltpu.VMEM((4, 2, 2, 4, 2, D, D), jnp.bfloat16),
            pltpu.VMEM((4, 2, 2, 2, 4, D, D), jnp.bfloat16),
            pltpu.VMEM((2, PROMPT, ROWS), jnp.float32),
            pltpu.VMEM((2, 8, ROWS), jnp.float32),
            pltpu.VMEM((TOKENS, ROWS), jnp.float32),
            pltpu.VMEM((HEADS_KV * TILES, D, ROWS), jnp.float32),
            pltpu.VMEM((HEADS_KV * TILES, 2, 8, ROWS), jnp.float32),
            dma((6,)),
            dma((3, 2)), dma((3, 2)),
            dma((3, 2, 2)), dma((3, 2, 2)),
            dma((4, 3)), dma((4, 3)),
            dma((4, 3)), dma((4, 3)),
            dma((4, 2, 3)), dma((4, 2, 3)),
            dma((4, 3)), dma((4, 3)),
            dma((2, 4)), dma((2, 4)),
            dma((4,)), dma((4,)),
            dma((3, 2, 2)), dma((3, 2, 2)),
        ],
        compiler_params=pltpu.CompilerParams(
            collective_id=0, has_side_effects=True, vmem_limit_bytes=56 * 2**20
        ),
        cost_estimate=pl.CostEstimate(flops=14_000_000_000, bytes_accessed=8_000_000, transcendentals=27_000_000),
    )(scales, key_codes, value_codes, lengths, queries[0], own_keys[0], own_values[0])
    return out[None]


def solution(mesh):
    placed = (
        P(("blk", "uly"), None, None),
        P(("blk", "uly"), None, None),
        P(("blk", "uly"), None, None),
        P("blk", "uly"),
        P("blk", "uly"),
        P("blk", "uly", None),
        P(("blk", "uly")),
    )
    return jax.shard_map(
        body, mesh=mesh, in_specs=placed, out_specs=P(("blk", "uly"), None, None), check_vma=False
    )
```

time: 72.8 us -> 58.7 us (0.81)
  Pallas kernels: 68.1 us -> 56.2 us
  local copies, waits for them, and re-layouts: 3.86 us -> 1.67 us
    pallas_call x1, Pallas kernels: 68.1 us -> 56.2 us  [body(): pl.pallas_call(attend, out_shape=pltpu.VMEM((LENGTH, width), jnp.bfloat16...]
    unnamed x1, local copies, waits for them, and re-layouts: 3.86 us -> 1.67 us
where the time goes in v3:
time: 58.7 us; the launch traced here: 58.6 us
  Pallas kernels  56.2 us (96%)
  local copies, waits for them, and re-layouts  1.67 us (3%)
  between operations  0.66 us (1%)
    pallas_call x1, Pallas kernels, body(): pl.pallas_call(attend, out_shape=pltpu.VMEM((LENGTH, width), jnp.bfloat16...  56.2 us
    unnamed x1, local copies, waits for them, and re-layouts  1.67 us

profile of v3, /device:TPU:1, one launch (start us, length us, event | category | flops | bytes accessed | tf_op | source)
XLA Modules:
  0.0 58.6 jit_solution(16098680871723409529)
XLA Ops:
  0.7 56.2 %shard_map.73 = bf16[192,8192]{1,0:T(8,128)(2,1)S(1)} custom-call(bf16[2,128]{1,0:T(2,128)(2,1)} %bitcast.11, bf16[128,128]{1,0:T(8,128)(2,1)} %kc_hbm.1, bf16[128,128]{1,0:T(8,128)(2,1)} %vc_hbm.1, s32[1]{0:T(128)S(6)} %copy.10.lengths_ref, bf16[192,8192]{1,0:T(8,128)(2,1)} %bitcast.8, bf16[192,1024]{1,0:T(8,128)(2,1)} %bitcast.9, bf16[192,1024]{1,0:T(8,128)(2,1)} %bitcast.10), custom_call_target="tpu_custom_call" | custom-call | flops 14000000000 | bytes 8000000 | tf_op jit(solution)/shard_map/pallas_call | solution.py:411
  56.9 1.7 %copy.9 = bf16[1,192,8192]{2,1,0:T(8,128)(2,1)} copy(bf16[1,192,8192]{2,1,0:T(8,128)(2,1)S(1)} %bitcast.7) | data formatting | bytes 6291456

commit v4 on v3

--- a/solution.py
+++ b/solution.py
@@ -20,7 +20,7 @@
 TILES = 6
 SCALE = math.log2(math.e) / math.sqrt(D)
 STEPS = (2, 1, 3)
-NEAR = 96
+NEAR = 64
 
 
 def dot_t(a, b):
@@ -91,7 +91,7 @@
         )
 
     def rows(p):
-        return pl.ds(0, D if isinstance(p, int) and p == 0 else NEAR)
+        return pl.ds(0, D if isinstance(p, int) and p % 3 == 0 else NEAR)
 
     far = pl.ds(NEAR, D - NEAR)
 
@@ -107,15 +107,15 @@
     def x_out(i):
         to = along_x((3, 1, 2)[i])
         return [
-            move(kbuf.at[x, yl, core, z, yh, pl.ds(0, NEAR)], x_send.at[i, 0], x_recv.at[i, 0], to),
-            move(vbuf.at[x, yl, core, yh, z, pl.ds(0, NEAR)], x_send.at[i, 1], x_recv.at[i, 1], to),
+            move(kbuf.at[x, yl, core, z, yh, rows(i + 1)], x_send.at[i, 0], x_recv.at[i, 0], to),
+            move(vbuf.at[x, yl, core, yh, z, rows(i + 1)], x_send.at[i, 1], x_recv.at[i, 1], to),
         ]
 
     def x_in(p):
         xp = plane(p)
         return [
-            move(kbuf.at[xp, yl, core, z, yh, pl.ds(0, NEAR)], x_send.at[p - 1, 0], x_recv.at[p - 1, 0], sibling),
-            move(vbuf.at[xp, yl, core, yh, z, pl.ds(0, NEAR)], x_send.at[p - 1, 1], x_recv.at[p - 1, 1], sibling),
+            move(kbuf.at[xp, yl, core, z, yh, rows(p)], x_send.at[p - 1, 0], x_recv.at[p - 1, 0], sibling),
+            move(vbuf.at[xp, yl, core, yh, z, rows(p)], x_send.at[p - 1, 1], x_recv.at[p - 1, 1], sibling),
         ]
 
     def far_out(i, a):
@@ -216,7 +216,7 @@
         for i in ((0,), (1, 2))[a]:
             v2_in(0, i).wait_recv()
             sv(i, core).start()
-        for i in range(3):
+        for i in range(2):
             start(far_out(i, a))
 
     def have_first(a):
@@ -225,12 +225,14 @@
 
     def share_later(p, a):
         arrive([k2_in(p, a, i) for i in (1, 2, 0)])
-        kf, vf = far_in(p, a)
-        kf.wait_recv()
+        through_x = not (isinstance(p, int) and p == 3)
+        if through_x:
+            far_in(p, a)[0].wait_recv()
         ks, vs = share(p, a, core)
         ks.start()
         arrive([v2_in(p, i) for i in ((0,), (1, 2))[a]])
-        vf.wait_recv()
+        if through_x:
+            far_in(p, a)[1].wait_recv()
         vs.start()
 
     def have_later(p, a):
@@ -282,41 +284,48 @@
             acc_ref[g * TILES + t] = jnp.dot(turned[:, :n], weighed[t], preferred_element_type=jnp.float32)
         return carry
 
-    def key_blocks(xp, hd):
-        return [kbuf[xp, hd, c, zz, hh] for c in range(2) for zz in range(4) for hh in range(2)]
-
-    def value_blocks(xp, hd):
-        return [vbuf[xp, hd, c, hh, zz] for c in range(2) for zz in range(4) for hh in range(2)]
+    def key_blocks(xp, hd, side):
+        cores = range(2) if side is None else (side,)
+        return [kbuf[xp, hd, c, zz, hh] for c in cores for zz in range(4) for hh in range(2)]
+
+    def value_blocks(xp, hd, side):
+        cores = range(2) if side is None else (side,)
+        return [vbuf[xp, hd, c, hh, zz] for c in cores for zz in range(4) for hh in range(2)]
 
     per = CHUNK // D
 
-    def scores(p, a, t, slot):
+    def scores(p, a, t, slot, side=None):
         xp, hd = plane(p), head(a)
         g = xp * 2 + hd
         q = queries(g, t)
-        blocks = key_blocks(xp, hd)
+        blocks = key_blocks(xp, hd, side)
         top = state_ref[g * TILES + t, 0]
-        for c in range(PROMPT // CHUNK):
+        for c in range(len(blocks) // per):
             keys = jnp.concatenate(blocks[c * per : (c + 1) * per], axis=0)
             s = dot_t(jnp.concatenate([keys, keys], axis=1), q)
             s_ref[slot, c * CHUNK : (c + 1) * CHUNK] = s
             top = jnp.maximum(top, jnp.max(s.reshape(CHUNK // 8, 8, ROWS), axis=0))
         m_ref[slot] = jnp.broadcast_to(jnp.max(top, axis=0, keepdims=True), (8, ROWS))
 
-    def values(p, a, t, slot):
+    def values(p, a, t, slot, side=None, last=True):
         xp, hd = plane(p), head(a)
         g = xp * 2 + hd
         hh, j = t // 3, t % 3
-        blocks = value_blocks(xp, hd)
+        blocks = value_blocks(xp, hd, side)
         top = m_ref[slot]
         shrink = jnp.exp2(state_ref[g * TILES + t, 0] - top)
         total = state_ref[g * TILES + t, 1] * shrink
         acc = acc_ref[g * TILES + t] * shrink[:1]
-        for c in range(PROMPT // CHUNK):
+        for c in range(len(blocks) // per):
             w = jnp.exp2(s_ref[slot, c * CHUNK : (c + 1) * CHUNK] - top[:1])
             total = total + jnp.sum(w.reshape(CHUNK // 8, 8, ROWS), axis=0)
             turned = jnp.concatenate(blocks[c * per : (c + 1) * per], axis=1)
             acc = acc + jnp.dot(turned, w.astype(jnp.bfloat16), preferred_element_type=jnp.float32)
+        if not last:
+            acc_ref[g * TILES + t] = acc
+            state_ref[g * TILES + t, 0] = top
+            state_ref[g * TILES + t, 1] = total
+            return
         token = lax.broadcasted_iota(jnp.int32, (1, ROWS), 1) % TOKENS + j * TOKENS
         factor = jnp.where(token < length, 1.0 / jnp.sum(total, axis=0, keepdims=True), 0.0)
         out = (acc * factor).T.astype(jnp.bfloat16)
@@ -325,40 +334,58 @@
 
     for load in loads[3:]:
         load.wait()
-    lax.fori_loop(0, 2, own_head, 0)
+    lax.fori_loop(0, 4, own_head, 0)
     second_own(0)
     start_first(1)
-    lax.fori_loop(2, 5, own_head, 0)
+    lax.fori_loop(4, HEADS_KV, own_head, 0)
     share_first(0)
     second_other(0)
-    lax.fori_loop(5, HEADS_KV, own_head, 0)
-    second_own(1)
-    have_first(0)
-    scores(0, 0, 0, 0)
+
+    halves = [(a, t, side) for a in range(2) for side in range(2) for t in range(TILES)]
+    cores = (core, other)
+
+    def work_first():
+        for v, (a, t, side) in enumerate(halves):
+            if v == 5:
+                have_first(0)
+                start_first(2)
+                start_first(3)
+            if v == 3:
+                second_own(1)
+            if v == 8:
+                second_other(1)
+            if v == 11:
+                share_first(1)
+            if v == 14:
+                start_second(2)
+            if v == 21:
+                start_second(3)
+            if v == 17:
+                have_first(1)
+            if v == 18:
+                share_later(1, 0)
+            if v == 23:
+                have_later(1, 0)
+                scores(1, 0, 0, 0)
+            else:
+                aa, tt, ss = halves[v + 1]
+                scores(0, aa, tt, (v + 1) % 2, cores[ss])
+            values(0, a, t, v % 2, cores[side], side == 1)
+
+    scores(0, 0, 0, 0, core)
 
     def work(p, place):
         for u in range(2 * TILES):
             a, t = u // TILES, u % TILES
-            if place == 0:
-                if u == 0:
-                    start_first(2)
-                    start_first(3)
-                if u == 2:
-                    second_other(1)
-                if u == 3:
-                    share_first(1)
-                if u == 5:
-                    have_first(1)
-                    start_second(2)
-                if u == 9:
-                    start_second(3)
-            else:
-                if u == 1:
-                    share_later(p, 1)
-                if u == 5:
-                    have_later(p, 1)
-            if place < 2 and u == 7:
-                share_later(p + 1, 0)
+            if u == 0:
+                share_later(p, 1)
+            if u == 5:
+                have_later(p, 1)
+            if place == 1 and u == 6:
+                for was in (1, 2):
+                    @pl.when(p == was)
+                    def _():
+                        share_later(was + 1, 0)
             if place < 2 and u == 11:
                 have_later(p + 1, 0)
             if u < 11:
@@ -371,7 +398,7 @@
         work(p, 1)
         return carry
 
-    work(0, 0)
+    work_first()
     lax.fori_loop(1, 3, planes, 0)
     work(3, 2)
 
@@ -388,18 +415,16 @@
     for i in range(3):
         sent(x_out(i))
         for a in range(2):
-            sent(far_out(i, a))
+            if i < 2:
+                sent(far_out(i, a))
     for i in range(4):
         sent([sk(0, i, core), sk(1, i, core), sv(i, core)])
     settle(0)
 
-    def settle_later(p, carry):
+    for p in range(1, 4):
         settle(p)
         for a in range(2):
             sent(share(p, a, core))
-        return carry
-
-    lax.fori_loop(1, 4, settle_later, 0)
 
 
 def body(queries, own_keys, own_values, key_codes, value_codes, code_scales, lengths):
@@ -429,7 +454,7 @@
             pltpu.VMEM((HEADS_KV * TILES, 2, 8, ROWS), jnp.float32),
             dma((6,)),
             dma((3, 2)), dma((3, 2)),
-            dma((3, 2, 2)), dma((3, 2, 2)),
+            dma((2, 2, 2)), dma((2, 2, 2)),
             dma((4, 3)), dma((4, 3)),
             dma((4, 3)), dma((4, 3)),
             dma((4, 2, 3)), dma((4, 2, 3)),

time: 58.7 us -> 56.5 us (0.963)
  Pallas kernels: 56.2 us -> 54.1 us
    pallas_call x1, Pallas kernels: 56.2 us -> 54.1 us  [body(): pl.pallas_call(attend, out_shape=pltpu.VMEM((LENGTH, width), jnp.bfloat16...]
where the time goes in v4:
time: 56.5 us; the launch traced here: 56.4 us
  Pallas kernels  54.1 us (96%)
  local copies, waits for them, and re-layouts  1.67 us (3%)
  between operations  0.66 us (1%)
    pallas_call x1, Pallas kernels, body(): pl.pallas_call(attend, out_shape=pltpu.VMEM((LENGTH, width), jnp.bfloat16...  54.1 us
    unnamed x1, local copies, waits for them, and re-layouts  1.67 us

profile of v4, /device:TPU:1, one launch (start us, length us, event | category | flops | bytes accessed | tf_op | source)
XLA Modules:
  0.0 56.4 jit_solution(13684219300692192536)
XLA Ops:
  0.7 54.1 %shard_map.73 = bf16[192,8192]{1,0:T(8,128)(2,1)S(1)} custom-call(bf16[2,128]{1,0:T(2,128)(2,1)} %bitcast.11, bf16[128,128]{1,0:T(8,128)(2,1)} %kc_hbm.1, bf16[128,128]{1,0:T(8,128)(2,1)} %vc_hbm.1, s32[1]{0:T(128)S(6)} %copy.10.lengths_ref, bf16[192,8192]{1,0:T(8,128)(2,1)} %bitcast.8, bf16[192,1024]{1,0:T(8,128)(2,1)} %bitcast.9, bf16[192,1024]{1,0:T(8,128)(2,1)} %bitcast.10), custom_call_target="tpu_custom_call" | custom-call | flops 14000000000 | bytes 8000000 | tf_op jit(solution)/shard_map/pallas_call | solution.py:436
  54.7 1.7 %copy.9 = bf16[1,192,8192]{2,1,0:T(8,128)(2,1)} copy(bf16[1,192,8192]{2,1,0:T(8,128)(2,1)S(1)} %bitcast.7) | data formatting | bytes 6291456
